TPU v7x, 32 devices: a whole 2x2x4 slice. The times are simulated.
32 devices in a mesh: ep: 2 (over x), kv: 16 (over z, y, core).
Axes of the slice: x: 2, y: 2, z: 4, core: 2. Of those that a mesh axis runs over, the one named last changes fastest.
Arguments:
- queries: bfloat16 [32, 1536], P(('ep', 'kv'))
- key_cache_pages: bfloat16 [512, 64, 512], P(('ep', 'kv'))
- value_cache_pages: bfloat16 [512, 64, 512], P(('ep', 'kv')), may hold values from -5 to 5
- page_table: int32 [32, 65], replicated, may hold values from 0 to 511, as said below
- lengths: int32 [32], replicated, may hold values from 2 to 32768, as said below
- sink_head_logits: float32 [24], replicated, may hold values from -1 to 5
- output_weight: bfloat16 [1536, 1536], replicated, may hold values from -0.15625 to 0.15625
- decode_stream: bfloat16 [32, 1536], P(('ep', 'kv')), may hold values from -6 to 6
- prefill_stream: bfloat16 [4064, 1536], P(('ep', 'kv')), may hold values from -6 to 6
- norm_gain: float32 [1536], replicated, may hold values from 0.1 to 1.9
- expert_gate: bfloat16 [16, 1536, 512], P('kv'), may hold values from -0.15625 to 0.15625
- expert_up: bfloat16 [16, 1536, 512], P('kv'), may hold values from -0.15625 to 0.15625
- expert_down: bfloat16 [16, 512, 1536], P('kv'), may hold values from -0.25 to 0.25
- route_ids: int32 [4096, 8], P(('ep', 'kv')), may hold values from 0 to 15, all different within a row; in each aligned block of 128 rows (0 to 127, 128 to 255, ...) at most 96 rows name the same one
- route_gates: float32 [4096, 8], P(('ep', 'kv')), may hold values from 0.03 to 0.6
Outputs:
- layer_out: bfloat16 [4096, 1536], P(('ep', 'kv'))
Inputs may be any that keep to these rules, and one draw needn't show every extreme that they name: In each aligned block of 16 requests, 1 request, which ones drawn from the seed, have lengths of 4096 or more; the others have lengths of at most 512. `page_table`: no two live slots name the same page. Every slot of a request in aligned block g of 16 requests names a page among g * 16 * 16 to (g + 1) * 16 * 16 - 1. `route_ids`: every row names 8 different experts; among the 128 rows of one device no expert is named by more than 96 rows.
All inputs are finite; a program needn't handle non-finite values.
Results may differ from a plain program's by a relative error of at most 0.0053.
Values may be sent and summed in bfloat16 or wider, within the bound.
A program may use at most 128 MiB of HBM per device.

v0:
```python
import jax
import jax.numpy as jnp
from jax import lax
from jax.sharding import PartitionSpec as P

QUERY_HEADS = 24
KEY_VALUE_HEADS = 8
HEAD_WIDTH = 64
TOPK = 8
WINDOW = 4096
lowest = -1e30


def joined(shard, axis, combine):
    everything = jax.tree.map(lambda part: lax.all_gather(part, axis), shard)
    leading = jax.tree.map(lambda part: part[0], everything)

    def step(k, so_far):
        return combine(so_far, jax.tree.map(lambda part: part[k], everything))

    return lax.fori_loop(1, lax.axis_size(axis), step, leading)


def merge_partials(first_part, second_part):
    max_first, total_first, out_first = first_part
    max_second, total_second, out_second = second_part
    highest = jnp.maximum(max_first, max_second)
    weight_first = jnp.exp(max_first - highest)
    weight_second = jnp.exp(max_second - highest)
    merged_total = total_first * weight_first + total_second * weight_second
    merged_out = out_first * jnp.repeat(weight_first, HEAD_WIDTH, axis=1) + out_second * jnp.repeat(
        weight_second, HEAD_WIDTH, axis=1
    )
    return (highest, merged_total, merged_out)


def rms_rows(stream):
    widened = stream.astype(jnp.float32)
    return widened * lax.rsqrt(jnp.mean(widened * widened, axis=-1, keepdims=True) + 1e-06)


def on_device(
    queries,
    key_cache_pages,
    value_cache_pages,
    page_table,
    lengths,
    sink_head_logits,
    output_weight,
    decode_stream,
    prefill_stream,
    norm_gain,
    expert_gate,
    expert_up,
    expert_down,
    route_ids,
    route_gates,
):
    device_index = lax.axis_index(("ep", "kv"))
    group_index = lax.axis_index("ep")
    member_index = lax.axis_index("kv")
    request_count = lax.axis_size("kv")
    local_pool_index = key_cache_pages.shape[0]
    page_length = key_cache_pages.shape[1]
    win_slots = page_table.shape[1]
    group_width = QUERY_HEADS // KEY_VALUE_HEADS
    score_scale = HEAD_WIDTH ** (-0.5)
    query_rows_full = lax.all_gather(queries, "kv", axis=0, tiled=True)
    group_first = group_index * request_count
    group_table = lax.dynamic_slice_in_dim(page_table, group_first, request_count, 0)
    group_lengths = lax.dynamic_slice_in_dim(lengths, group_first, request_count, 0)
    window_start = jnp.maximum(group_lengths - WINDOW, 0)
    first_page = window_start // page_length
    slot_index = jnp.arange(win_slots, dtype=jnp.int32)
    live_slot = (first_page[:, None] + slot_index[None, :]) * page_length < group_lengths[:, None]
    local_id = group_table - device_index * local_pool_index
    mine = live_slot & (local_id >= 0) & (local_id < local_pool_index)
    target = jnp.where(mine, local_id, local_pool_index).reshape(-1)
    request_grid = jnp.broadcast_to(
        jnp.arange(request_count, dtype=jnp.int32)[:, None], (request_count, win_slots)
    ).reshape(-1)
    slot_grid = jnp.broadcast_to(slot_index[None, :], (request_count, win_slots)).reshape(-1)
    page_request = (
        jnp.full((local_pool_index,), request_count, jnp.int32)
        .at[target]
        .set(request_grid, mode="drop")
    )
    page_slot = jnp.zeros((local_pool_index,), jnp.int32).at[target].set(slot_grid, mode="drop")
    page_used = page_request < request_count
    clamped_request = jnp.minimum(page_request, request_count - 1)
    page_first = (first_page[clamped_request] + page_slot) * page_length
    positions = page_first[:, None] + jnp.arange(page_length, dtype=jnp.int32)[None, :]
    in_window = (
        page_used[:, None]
        & (positions >= window_start[clamped_request][:, None])
        & (positions < group_lengths[clamped_request][:, None])
    )
    queries_of_page = query_rows_full[clamped_request].reshape(
        local_pool_index, KEY_VALUE_HEADS, group_width, HEAD_WIDTH
    )
    key_pieces = key_cache_pages.reshape(local_pool_index, page_length, KEY_VALUE_HEADS, HEAD_WIDTH)
    value_pieces = value_cache_pages.reshape(
        local_pool_index, page_length, KEY_VALUE_HEADS, HEAD_WIDTH
    )
    scores = (
        jnp.einsum(
            "pgqd,ptgd->pgqt", queries_of_page, key_pieces, preferred_element_type=jnp.float32
        )
        * score_scale
    )
    mask_full = in_window[:, None, None, :]
    scores = jnp.where(mask_full, scores, lowest)
    slot_max = jnp.max(scores, axis=-1)
    weights = jnp.where(mask_full, jnp.exp(scores - slot_max[..., None]), 0.0).astype(jnp.bfloat16)
    slot_total = jnp.sum(weights.astype(jnp.float32), axis=-1).reshape(
        local_pool_index, QUERY_HEADS
    )
    slot_out = jnp.einsum(
        "pgqt,ptgd->pgqd", weights, value_pieces, preferred_element_type=jnp.float32
    ).reshape(local_pool_index, QUERY_HEADS, HEAD_WIDTH)
    slot_max = jnp.where(
        page_used[:, None], slot_max.reshape(local_pool_index, QUERY_HEADS), lowest
    )
    owner = (page_request[None, :] == jnp.arange(request_count, dtype=jnp.int32)[:, None])[
        :, :, None
    ]
    request_max = jnp.max(jnp.where(owner, slot_max[None], lowest), axis=1)
    rescale = jnp.where(owner, jnp.exp(slot_max[None] - request_max[:, None]), 0.0)
    request_total = jnp.sum(rescale * slot_total[None], axis=1)
    request_out = jnp.einsum("rph,phd->rhd", rescale, slot_out).reshape(
        request_count, QUERY_HEADS * HEAD_WIDTH
    )
    merged_max, merged_total, merged_out = joined(
        (request_max, request_total, request_out), "kv", merge_partials
    )
    own_max = lax.dynamic_slice_in_dim(merged_max, member_index, 1, 0)
    own_total = lax.dynamic_slice_in_dim(merged_total, member_index, 1, 0)
    own_out = lax.dynamic_slice_in_dim(merged_out, member_index, 1, 0)
    sink_logit_row = sink_head_logits[None, :]
    ceiling = jnp.maximum(own_max, sink_logit_row)
    keep_factor = jnp.exp(own_max - ceiling)
    denominator = own_total * keep_factor + jnp.exp(sink_logit_row - ceiling)
    attended = (own_out * jnp.repeat(keep_factor / denominator, HEAD_WIDTH, axis=1)).astype(
        jnp.bfloat16
    )
    decode_hidden = (
        decode_stream.astype(jnp.float32)
        + jnp.dot(attended, output_weight, preferred_element_type=jnp.float32)
    ).astype(jnp.bfloat16)
    gain_row = norm_gain[None, :]
    normed_prefill = (rms_rows(prefill_stream) * gain_row).astype(jnp.bfloat16)
    normed_decode = (rms_rows(decode_hidden) * gain_row).astype(jnp.bfloat16)
    mixed_rows = jnp.concatenate([prefill_stream, decode_hidden], axis=0)
    residual = mixed_rows.astype(jnp.float32)
    row_count = mixed_rows.shape[0]
    width = mixed_rows.shape[1]
    expert_count = lax.axis_size("kv")
    capacity = min(row_count, 3 * row_count * TOPK // (2 * expert_count))
    pair_expert = route_ids.reshape(-1)
    onehot = (pair_expert[:, None] == jnp.arange(expert_count, dtype=jnp.int32)[None, :]).astype(
        jnp.int32
    )
    pair_rank = jnp.sum((jnp.cumsum(onehot, axis=0) - onehot) * onehot, axis=1)
    pair_slot = pair_expert * capacity + pair_rank
    pair_row = jnp.arange(row_count * TOPK, dtype=jnp.int32) // TOPK
    slot_row = (
        jnp.full((expert_count * capacity,), row_count, jnp.int32).at[pair_slot].set(pair_row)
    )
    normed = jnp.concatenate([normed_prefill, normed_decode], axis=0)
    extended = jnp.concatenate([normed, jnp.zeros((1, width), jnp.bfloat16)], axis=0)
    outgoing = extended[slot_row].reshape(expert_count, capacity, width)
    slot_block = lax.all_to_all(outgoing, "kv", split_axis=0, concat_axis=0, tiled=True)
    gate_part = jnp.einsum(
        "scd,df->scf", slot_block, expert_gate[0], preferred_element_type=jnp.float32
    )
    up_part = jnp.einsum(
        "scd,df->scf", slot_block, expert_up[0], preferred_element_type=jnp.float32
    )
    hidden = (jax.nn.silu(gate_part) * up_part).astype(jnp.bfloat16)
    processed = jnp.einsum(
        "scf,fd->scd", hidden, expert_down[0], preferred_element_type=jnp.float32
    ).astype(jnp.bfloat16)
    returned = lax.all_to_all(processed, "kv", split_axis=0, concat_axis=0, tiled=True).reshape(
        expert_count * capacity, width
    )
    pair_values = returned[pair_slot]
    weighted = (
        pair_values.reshape(row_count, TOPK, width).astype(jnp.float32) * route_gates[:, :, None]
    )
    combined = jnp.sum(weighted, axis=1)
    return (residual + combined).astype(jnp.bfloat16)


def solution(mesh):
    in_specs = (
        P(("ep", "kv"), None),
        P(("ep", "kv"), None, None),
        P(("ep", "kv"), None, None),
        P(),
        P(),
        P(),
        P(),
        P(("ep", "kv"), None),
        P(("ep", "kv"), None),
        P(),
        P("kv", None, None),
        P("kv", None, None),
        P("kv", None, None),
        P(("ep", "kv"), None),
        P(("ep", "kv"), None),
    )
    out_specs = P(("ep", "kv"), None)
    return jax.shard_map(
        on_device, mesh=mesh, in_specs=in_specs, out_specs=out_specs, check_vma=False
    )
```

profile of v0, /device:TPU:13, one launch (start us, length us, event | category | flops | bytes accessed | tf_op | source)
XLA Modules:
  0.0 396.2 jit_solution(12079475339717835462)
XLA Ops:
  8.4 6.4 %scatter_custom_fusion = s32[16]{0:T(128)S(1)} fusion(s32[1040]{0:T(1024)S(1)} %fusion.43, s32[1040]{0:T(1024)S(1)} %reshape.312, s32[]{:T(128)} %constant.108.clone.1), kind=kCustom, calls=%fused_computation.114 | custom fusion | bytes 68 | tf_op jit(solution)/shard_map/scatter | solution.py:86
  16.4 6.4 %scatter_custom_fusion.1 = s32[16]{0:T(128)S(1)} fusion(s32[1040]{0:T(1024)S(1)} %fusion.43, s32[1040]{0:T(1024)S(1)} %reshape.320, s32[]{:T(128)} %constant.107.clone.1), kind=kCustom, calls=%fused_computation.111 | custom fusion | bytes 68 | tf_op jit(solution)/shard_map/scatter | solution.py:88
  23.5 16.1 %all-gather.2 = bf16[16,1,1536]{2,1,0:T(2,128)(2,1)S(1)} all-gather(bf16[1,1,1536]{2,1,0:T(2,128)(2,1)} %bitcast.96), channel_id=1, replica_groups=mesh['ep'=2,'kv'=16] {'kv'}, dimensions={0}, use_global_device_ids=true | all-gather | bytes 52224 | tf_op jit(solution)/shard_map/all_gather | solution.py:68
  40.4 2.1 reshape.251
  42.5 3.9 reshape.253
  46.5 2.9 fusion.63
  49.5 2.4 fusion.5
  54.4 21.7 %all-gather.1 = f32[256,24]{1,0:T(8,128)S(1)} all-gather(f32[16,24]{1,0:T(8,128)S(1)} %copy.72), channel_id=3, replica_groups=mesh['ep'=2,'kv'=16] {'kv'}, dimensions={0}, use_global_device_ids=true | all-gather | bytes 26112 | tf_op jit(solution)/shard_map/all_gather | solution.py:15
  76.1 18.0 %all-gather = f32[256,24]{1,0:T(8,128)S(1)} all-gather(f32[16,24]{1,0:T(8,128)S(1)} %copy.70), channel_id=2, replica_groups=mesh['ep'=2,'kv'=16] {'kv'}, dimensions={0}, use_global_device_ids=true | all-gather | bytes 26112 | tf_op jit(solution)/shard_map/all_gather | solution.py:15
  94.1 4.5 %reduce-window.6 = s32[16,8,128]{2,1,0:T(8,128)S(1)} reduce-window(s32[16,8,128]{2,1,0:T(8,128)S(1)} %fusion.31, s32[]{:T(128)} %constant.107.clone.1), window={size=1x1x128 pad=0_0x0_0x127_0}, to_apply=%region_10.11 | reduce-window | flops 2080768 | bytes 131076 | tf_op jit(solution)/shard_map/reduce-window
  99.3 4.3 %scatter_custom_fusion.2 = s32[1536]{0:T(1024)S(1)} fusion(s32[1024]{0:T(1024)S(1)} %bitcast.94, s32[1024]{0:T(1024)S(1)} %add_select_fusion, s32[]{:T(128)} %constant.127.clone.1), kind=kCustom, calls=%fused_computation.90 | custom fusion | bytes 6148 | tf_op jit(solution)/shard_map/scatter | solution.py:167
  105.0 21.4 %while.19 = (s32[]{:T(128)}, f32[16,24]{1,0:T(8,128)S(1)}, f32[16,24]{1,0:T(8,128)S(1)}, f32[16,1536]{1,0:T(8,128)S(1)}, f32[16,16,24]{2,1,0:T(8,128)S(1)}, /*in...) while((s32[]{:T(128)}, f32[16,24]{1,0:T(8,128)S(1)}, ...), condition=%wide.region_7.8_spmd, body=%wide.region_6.7_spmd.sunk | while | flops 76037 | bytes 1096855 | solution.py:21
  105.4 0.9 fusion.72
  106.9 0.9 fusion.72
  108.3 0.9 fusion.72
  109.7 0.9 fusion.72
  112.6 0.9 fusion.72
  114.0 0.9 fusion.72
  115.4 0.9 fusion.72
  116.8 0.9 fusion.72
  119.7 0.9 fusion.72
  121.1 0.9 fusion.72
  126.5 3.7 multiply_reduce_fusion.1
  131.1 6.2 %gather_fusion.4 = bf16[1536,1536]{1,0:T(8,128)(2,1)} fusion(bf16[129,1536]{1,0:T(8,128)(2,1)S(1)} %maximum_maximum_fusion, s32[2048]{0:T(1024)S(1)} %pad_clamp_fusion), kind=kCustom, calls=%fused_computation.4 | custom fusion | bytes 9443328 | tf_op jit(solution)/shard_map/gather | solution.py:171
  137.3 111.5 %all_to_all.10 = bf16[16,96,1536]{2,1,0:T(8,128)(2,1)S(1)} all-to-all(bf16[16,96,1536]{2,1,0:T(8,128)(2,1)} %bitcast.86), channel_id=1, replica_groups=mesh['ep'=2,'kv'=16] {'kv'}, dimensions={0} | all-to-all | bytes 9437184 | tf_op jit(solution)/shard_map/all_to_all | solution.py:172
  248.8 2.2 copy-done.1
  251.0 4.2 %fusion.10 = f32[16,96,512]{2,1,0:T(8,128)} fusion(bf16[16,96,1536]{2,1,0:T(8,128)(2,1)S(1)} %all_to_all.10, bf16[1,1536,512]{2,1,0:T(8,128)(2,1)S(1)} %copy-done.9), kind=kOutput, calls=%fused_computation.28 | convolution fusion | flops 2415919104 | bytes 9437184 | tf_op jit(solution)/shard_map/scd,df->scf/dot_general | solution.py:176
  255.2 9.6 %convolution_convert_fusion = bf16[16,96,1536]{2,1,0:T(8,128)(2,1)} fusion(bf16[1,512,1536]{2,1,0:T(8,128)(2,1)S(1)} %copy-done, f32[16,96,512]{2,1,0:T(8,128)} %fusion.10, bf16[16,96,1536]{2,1,0:T(8,128)(2,1)} %copy-done.1, bf16[1,1536,512]{2,1,0:T(8,128)(2,1)} %param.27), kind=kOutput, calls=%fused_computation.19 | convolution fusion | flops 4838916096 | bytes 15728640 | tf_op jit(solution)/shard_map/scf,fd->scd/dot_general | solution.py:180
  264.8 5.0 %all-to-all-start.1 = ((bf16[16,96,1536]{2,1,0:T(8,128)(2,1)}), bf16[16,96,1536]{2,1,0:T(8,128)(2,1)}, u32[]{:S(2)}, u32[]{:S(2)}) async-start(bf16[16,96,1536]{2,1,0:T(8,128)(2,1)} %convolution_convert_fusion), calls=%async_computation.1 | async-start | bytes 9437184 | tf_op jit(solution)/shard_map/all_to_all | solution.py:183
  270.0 103.6 %all-to-all-done.1 = bf16[16,96,1536]{2,1,0:T(8,128)(2,1)} async-done(((bf16[16,96,1536]{2,1,0:T(8,128)(2,1)}), bf16[16,96,1536]{2,1,0:T(8,128)(2,1)}, u32[]{:S(2)}, u32[]{:S(2)}) %all-to-all-start.1) | async-done | bytes 4718624 | tf_op jit(solution)/shard_map/all_to_all | solution.py:183
  373.6 10.2 %gather_fusion.5 = bf16[1024,1536]{1,0:T(8,128)(2,1)} fusion(bf16[1536,1536]{1,0:T(8,128)(2,1)} %bitcast.22, s32[1024]{0:T(1024)S(1)} %broadcast_clamp_fusion), kind=kCustom, calls=%fused_computation.5 | custom fusion | bytes 6295552 | tf_op jit(solution)/shard_map/gather | solution.py:186
  383.8 4.7 %fusion.3 = f32[128,1536]{1,0:T(8,128)S(1)} fusion(bf16[1024,1536]{1,0:T(8,128)(2,1)} %gather_fusion.5, f32[128,8]{1,0:T(8,128)S(1)} %copy.85), kind=kLoop, calls=%fused_computation.18 | loop fusion | flops 4521984 | bytes 3936256 | tf_op jit(solution)/shard_map/reduce_sum | solution.py:190
  (170 shorter events, 22.0 us)
Async XLA Ops:
  6.5 248.7 %copy-start = (bf16[1,512,1536]{2,1,0:T(8,128)(2,1)S(1)}, bf16[1,512,1536]{2,1,0:T(8,128)(2,1)}, u32[]{:S(2)}) copy-start(bf16[1,512,1536]{2,1,0:T(8,128)(2,1)} %param.29) | copy-start | bytes 4718596
  6.5 33.8 %copy-start.3 = (bf16[16,64,512]{2,1,0:T(8,128)(2,1)S(1)}, bf16[16,64,512]{2,1,0:T(8,128)(2,1)}, u32[]{:S(2)}) copy-start(bf16[16,64,512]{2,1,0:T(8,128)(2,1)} %param.18) | copy-start | bytes 3145732
  6.5 97.5 %all-gather.5.cloned.1.call-start = ((), (), s32[]{:S(2)}) async-start(), calls=%async_computation.2 | async-start | bytes 1671168 | tf_op jit(solution)/shard_map/all_gather | solution.py:15
  46.5 6.8 %copy-start.5 = (s32[128,8]{0,1:T(8,128)S(1)}, s32[128,8]{0,1:T(8,128)}, u32[]{:S(2)}) copy-start(s32[128,8]{0,1:T(8,128)} %param.30) | copy-start | bytes 12292
  49.4 54.2 %copy-start.2 = (bf16[127,1536]{1,0:T(8,128)(2,1)S(1)}, bf16[127,1536]{1,0:T(8,128)(2,1)}, u32[]{:S(2)}) copy-start(bf16[127,1536]{1,0:T(8,128)(2,1)} %param.25) | copy-start | bytes 1170436
  49.4 54.4 %copy-start.4 = (f32[1536]{0:T(1024)S(1)}, f32[1536]{0:T(1024)}, u32[]{:S(2)}) copy-start(f32[1536]{0:T(1024)} %param.26) | copy-start | bytes 18436
  104.9 21.4 %copy-start.8 = (f32[24]{0:T(128)S(1)}, f32[24]{0:T(128)}, u32[]{:S(2)}) copy-start(f32[24]{0:T(128)} %param.22) | copy-start | bytes 292
  104.9 21.6 %copy-start.6 = (bf16[1,1536]{1,0:T(2,128)(2,1)S(1)}, bf16[1,1536]{1,0:T(2,128)(2,1)}, u32[]{:S(2)}) copy-start(bf16[1,1536]{1,0:T(2,128)(2,1)} %param.24) | copy-start | bytes 9220
  137.3 113.7 %copy-start.9 = (bf16[1,1536,512]{2,1,0:T(8,128)(2,1)S(1)}, bf16[1,1536,512]{2,1,0:T(8,128)(2,1)}, u32[]{:S(2)}) copy-start(bf16[1,1536,512]{2,1,0:T(8,128)(2,1)} %param.28) | copy-start | bytes 4718596
  248.8 2.2 copy-start.1
  264.8 5.0 %copy-start.7 = (f32[128,8]{0,1:T(8,128)S(1)}, f32[128,8]{0,1:T(8,128)}, u32[]{:S(2)}) copy-start(f32[128,8]{0,1:T(8,128)} %param.31) | copy-start | bytes 12292
  264.8 108.7 %all-to-all-start.1 = ((bf16[16,96,1536]{2,1,0:T(8,128)(2,1)}), bf16[16,96,1536]{2,1,0:T(8,128)(2,1)}, u32[]{:S(2)}, u32[]{:S(2)}) async-start(bf16[16,96,1536]{2,1,0:T(8,128)(2,1)} %convolution_convert_fusion), calls=%async_computation.1 | async-start | bytes 9437184 | tf_op jit(solution)/shard_map/all_to_all | solution.py:183
Sparse Core Ops, SparseCore 0:
  53.3 41.7 all-gather.4
where the time goes:
time: 397 us; the launch traced here: 396 us
  blocking collectives  167 us (42%)
  waiting for transfers between devices  104 us (26%)
  local copies, waits for them, and re-layouts  54.5 us (14%)
  other arithmetic  27.7 us (7%)
  matrix products  22.9 us (6%)
  between operations  14.4 us (4%)
  starting transfers between devices  5.04 us (1%)
    all_to_all x1, blocking collectives, on_device(): lax.all_to_all(outgoing, 'kv', split_axis=0, concat_axis=0, tiled=True)  112 us
    all_to_all x1, waiting for transfers between devices, on_device(): lax.all_to_all(processed, 'kv', split_axis=0, concat_axis=0, tiled=True)  104 us
    all_gather x2, blocking collectives, joined(): everything = jax.tree.map(lambda part: lax.all_gather(part, axis), shard)  39.7 us
    all_gather x1, blocking collectives, on_device(): query_rows_full = lax.all_gather(queries, 'kv', axis=0, tiled=True)  16.1 us
    add x15, other arithmetic, merge_partials(): out_first * jnp.repeat(weight_first, HEAD_WIDTH, axis=1)  14 us
    gather x1, local copies, waits for them, and re-layouts, on_device(): pair_values = returned[pair_slot]  10.2 us
    dot_general x1, matrix products, on_device(): jnp.einsum('scf,fd->scd', hidden, expert_down[0], preferred_element_type=...  9.57 us
  transfers between devices with their start and end apart: 2, of which 1 were waited for; matrix products, arithmetic and copies ran while one was open for 3% of the time, Pallas kernels for 0%

commit v1 on v0

--- a/solution.py
+++ b/solution.py
@@ -65,7 +65,22 @@
     win_slots = page_table.shape[1]
     group_width = QUERY_HEADS // KEY_VALUE_HEADS
     score_scale = HEAD_WIDTH ** (-0.5)
-    query_rows_full = lax.all_gather(queries, "kv", axis=0, tiled=True)
+    ways, here, step_2 = (lax.axis_size("kv"), lax.axis_index("kv"), queries.shape[0])
+    dims = [n * ways if d == 0 else n for d, n in enumerate(queries.shape)]
+    query_rows_full = lax.dynamic_update_slice_in_dim(
+        jnp.zeros(dims, queries.dtype), queries, here * step_2, axis=0
+    )
+    going_up = going_down = queries
+    for far in range(1, ways // 2 + 1):
+        going_up = lax.ppermute(going_up, "kv", [(d, (d + 1) % ways) for d in range(ways)])
+        query_rows_full = lax.dynamic_update_slice_in_dim(
+            query_rows_full, going_up, (here - far) % ways * step_2, axis=0
+        )
+        if 2 * far < ways:
+            going_down = lax.ppermute(going_down, "kv", [(d, (d - 1) % ways) for d in range(ways)])
+            query_rows_full = lax.dynamic_update_slice_in_dim(
+                query_rows_full, going_down, (here + far) % ways * step_2, axis=0
+            )
     group_first = group_index * request_count
     group_table = lax.dynamic_slice_in_dim(page_table, group_first, request_count, 0)
     group_lengths = lax.dynamic_slice_in_dim(lengths, group_first, request_count, 0)

time: 397 us -> 415 us (1.045)
  starting transfers between devices: 5.04 us -> 25.6 us
  blocking collectives: 167 us -> 156 us
  waiting for transfers between devices: 104 us -> 110 us
    ppermute x0 -> x15, starting transfers between devices: none -> 20.4 us  [the longest x8 20.3 us: on_device(): lax.ppermute(going_up, 'kv', [(d, (d + 1) % ways) for d in range(ways)])]
    all_gather x1 -> x0, blocking collectives: 16.1 us -> none  [on_device(): query_rows_full = lax.all_gather(queries, 'kv', axis=0, tiled=True)]
    ppermute x0 -> x15, waiting for transfers between devices: none -> 6.46 us  [the longest x7 6.44 us: on_device(): lax.ppermute(going_down, 'kv', [(d, (d - 1) % ways) for d in range(ways)])]
    all_gather x2, blocking collectives: 39.7 us -> 45 us  [joined(): everything = jax.tree.map(lambda part: lax.all_gather(part, axis), shard)]
  transfers between devices with their start and end apart: 2 -> 17, of which waited for: 1 -> 6; matrix products, arithmetic and copies ran while one was open for 3% -> 9% of each run, Pallas kernels for 0% -> 0%
where the time goes in v1:
time: 415 us; the launch traced here: 413 us
  blocking collectives  156 us (38%)
  waiting for transfers between devices  110 us (27%)
  local copies, waits for them, and re-layouts  56 us (13%)
  other arithmetic  27.5 us (7%)
  starting transfers between devices  25.6 us (6%)
  matrix products  22.9 us (6%)
  between operations  14.7 us (4%)
    all_to_all x1, blocking collectives, on_device(): lax.all_to_all(outgoing, 'kv', split_axis=0, concat_axis=0, tiled=True)  111 us
    all_to_all x1, waiting for transfers between devices, on_device(): lax.all_to_all(processed, 'kv', split_axis=0, concat_axis=0, tiled=True)  104 us
    all_gather x2, blocking collectives, joined(): everything = jax.tree.map(lambda part: lax.all_gather(part, axis), shard)  45 us
    ppermute x8, starting transfers between devices, on_device(): lax.ppermute(going_up, 'kv', [(d, (d + 1) % ways) for d in range(ways)])  20.3 us
    add x15, other arithmetic, merge_partials(): out_first * jnp.repeat(weight_first, HEAD_WIDTH, axis=1)  14 us
    gather x1, local copies, waits for them, and re-layouts, on_device(): pair_values = returned[pair_slot]  10.2 us
    dot_general x1, matrix products, on_device(): jnp.einsum('scf,fd->scd', hidden, expert_down[0], preferred_element_type=...  9.56 us
  transfers between devices with their start and end apart: 17, of which 6 were waited for; matrix products, arithmetic and copies ran while one was open for 9% of the time, Pallas kernels for 0%

profile of v1, /device:TPU:13, one launch (start us, length us, event | category | flops | bytes accessed | tf_op | source)
XLA Modules:
  0.0 413.0 jit_solution(2284473237733503840)
XLA Ops:
  6.5 1.8 collective-permute-start
  10.1 6.4 %scatter_custom_fusion = s32[16]{0:T(128)S(1)} fusion(s32[1040]{0:T(1024)S(1)} %fusion.43, s32[1040]{0:T(1024)S(1)} %reshape.312, s32[]{:T(128)} %constant.188.clone.1), kind=kCustom, calls=%fused_computation.113 | custom fusion | bytes 68 | tf_op jit(solution)/shard_map/scatter | solution.py:101
  17.3 6.4 %scatter_custom_fusion.1 = s32[16]{0:T(128)S(1)} fusion(s32[1040]{0:T(1024)S(1)} %fusion.43, s32[1040]{0:T(1024)S(1)} %reshape.320, s32[]{:T(128)} %constant.187.clone.1), kind=kCustom, calls=%fused_computation.110 | custom fusion | bytes 68 | tf_op jit(solution)/shard_map/scatter | solution.py:103
  23.8 2.7 collective-permute-start.2
  27.9 2.6 collective-permute-start.4
  31.8 2.6 collective-permute-start.6
  35.8 2.6 collective-permute-start.8
  38.4 1.3 collective-permute-done.7
  39.7 2.6 collective-permute-start.10
  42.4 1.3 collective-permute-done.9
  43.7 2.6 collective-permute-start.12
  46.3 1.3 collective-permute-done.11
  47.6 2.6 collective-permute-start.14
  50.3 3.9 reshape.251
  54.2 2.1 reshape.253
  58.8 2.9 fusion.63
  61.8 2.4 fusion.5
  65.8 4.5 %reduce-window.6 = s32[16,8,128]{2,1,0:T(8,128)S(1)} reduce-window(s32[16,8,128]{2,1,0:T(8,128)S(1)} %fusion.31, s32[]{:T(128)} %constant.187.clone.1), window={size=1x1x128 pad=0_0x0_0x127_0}, to_apply=%region_10.11 | reduce-window | flops 2080768 | bytes 131076 | tf_op jit(solution)/shard_map/reduce-window
  71.0 4.3 %scatter_custom_fusion.2 = s32[1536]{0:T(1024)S(1)} fusion(s32[1024]{0:T(1024)S(1)} %bitcast.89, s32[1024]{0:T(1024)S(1)} %add_select_fusion, s32[]{:T(128)} %constant.219.clone.1), kind=kCustom, calls=%fused_computation.89 | custom fusion | bytes 6148 | tf_op jit(solution)/shard_map/scatter | solution.py:182
  76.7 26.2 %all-gather.1 = f32[256,24]{1,0:T(8,128)S(1)} all-gather(f32[16,24]{1,0:T(8,128)S(1)} %copy.72), channel_id=3, replica_groups=mesh['ep'=2,'kv'=16] {'kv'}, dimensions={0}, use_global_device_ids=true | all-gather | bytes 26112 | tf_op jit(solution)/shard_map/all_gather | solution.py:15
  102.8 18.8 %all-gather = f32[256,24]{1,0:T(8,128)S(1)} all-gather(f32[16,24]{1,0:T(8,128)S(1)} %copy.70), channel_id=2, replica_groups=mesh['ep'=2,'kv'=16] {'kv'}, dimensions={0}, use_global_device_ids=true | all-gather | bytes 26112 | tf_op jit(solution)/shard_map/all_gather | solution.py:15
  122.6 21.4 %while.19 = (s32[]{:T(128)}, f32[16,24]{1,0:T(8,128)S(1)}, f32[16,24]{1,0:T(8,128)S(1)}, f32[16,1536]{1,0:T(8,128)S(1)}, f32[16,16,24]{2,1,0:T(8,128)S(1)}, /*in...) while((s32[]{:T(128)}, f32[16,24]{1,0:T(8,128)S(1)}, ...), condition=%wide.region_7.8_spmd, body=%wide.region_6.7_spmd.sunk | while | flops 76037 | bytes 1096855 | solution.py:21
  144.2 3.7 multiply_reduce_fusion.1
  148.7 6.2 %gather_fusion.4 = bf16[1536,1536]{1,0:T(8,128)(2,1)} fusion(bf16[129,1536]{1,0:T(8,128)(2,1)S(1)} %maximum_maximum_fusion, s32[2048]{0:T(1024)S(1)} %pad_clamp_fusion), kind=kCustom, calls=%fused_computation.4 | custom fusion | bytes 9443328 | tf_op jit(solution)/shard_map/gather | solution.py:186
  154.9 110.6 %all_to_all.10 = bf16[16,96,1536]{2,1,0:T(8,128)(2,1)S(1)} all-to-all(bf16[16,96,1536]{2,1,0:T(8,128)(2,1)} %bitcast.82), channel_id=1, replica_groups=mesh['ep'=2,'kv'=16] {'kv'}, dimensions={0} | all-to-all | bytes 9437184 | tf_op jit(solution)/shard_map/all_to_all | solution.py:187
  265.5 2.2 copy-done.1
  267.7 4.2 %fusion.10 = f32[16,96,512]{2,1,0:T(8,128)} fusion(bf16[16,96,1536]{2,1,0:T(8,128)(2,1)S(1)} %all_to_all.10, bf16[1,1536,512]{2,1,0:T(8,128)(2,1)S(1)} %copy-done.10), kind=kOutput, calls=%fused_computation.28 | convolution fusion | flops 2415919104 | bytes 9437184 | tf_op jit(solution)/shard_map/scd,df->scf/dot_general | solution.py:191
  271.9 9.6 %convolution_convert_fusion = bf16[16,96,1536]{2,1,0:T(8,128)(2,1)} fusion(bf16[1,512,1536]{2,1,0:T(8,128)(2,1)S(1)} %copy-done, f32[16,96,512]{2,1,0:T(8,128)} %fusion.10, bf16[16,96,1536]{2,1,0:T(8,128)(2,1)} %copy-done.1, bf16[1,1536,512]{2,1,0:T(8,128)(2,1)} %param.27), kind=kOutput, calls=%fused_computation.19 | convolution fusion | flops 4838916096 | bytes 15728640 | tf_op jit(solution)/shard_map/scf,fd->scd/dot_general | solution.py:195
  281.5 5.2 %all-to-all-start.1 = ((bf16[16,96,1536]{2,1,0:T(8,128)(2,1)}), bf16[16,96,1536]{2,1,0:T(8,128)(2,1)}, u32[]{:S(2)}, u32[]{:S(2)}) async-start(bf16[16,96,1536]{2,1,0:T(8,128)(2,1)} %convolution_convert_fusion), calls=%async_computation.1 | async-start | bytes 9437184 | tf_op jit(solution)/shard_map/all_to_all | solution.py:198
  286.8 103.6 %all-to-all-done.1 = bf16[16,96,1536]{2,1,0:T(8,128)(2,1)} async-done(((bf16[16,96,1536]{2,1,0:T(8,128)(2,1)}), bf16[16,96,1536]{2,1,0:T(8,128)(2,1)}, u32[]{:S(2)}, u32[]{:S(2)}) %all-to-all-start.1) | async-done | bytes 4718624 | tf_op jit(solution)/shard_map/all_to_all | solution.py:198
  390.3 10.2 %gather_fusion.5 = bf16[1024,1536]{1,0:T(8,128)(2,1)} fusion(bf16[1536,1536]{1,0:T(8,128)(2,1)} %bitcast.21, s32[1024]{0:T(1024)S(1)} %broadcast_clamp_fusion), kind=kCustom, calls=%fused_computation.5 | custom fusion | bytes 6295552 | tf_op jit(solution)/shard_map/gather | solution.py:201
  400.6 4.7 %fusion.3 = f32[128,1536]{1,0:T(8,128)S(1)} fusion(bf16[1024,1536]{1,0:T(8,128)(2,1)} %gather_fusion.5, f32[128,8]{1,0:T(8,128)S(1)} %copy.85), kind=kLoop, calls=%fused_computation.18 | loop fusion | flops 4521984 | bytes 3936256 | tf_op jit(solution)/shard_map/reduce_sum | solution.py:205
  (217 shorter events, 35.3 us)
Async XLA Ops:
  6.5 265.4 %copy-start = (bf16[1,512,1536]{2,1,0:T(8,128)(2,1)S(1)}, bf16[1,512,1536]{2,1,0:T(8,128)(2,1)}, u32[]{:S(2)}) copy-start(bf16[1,512,1536]{2,1,0:T(8,128)(2,1)} %param.29) | copy-start | bytes 4718596
  6.5 47.7 %copy-start.3 = (bf16[16,64,512]{2,1,0:T(8,128)(2,1)S(1)}, bf16[16,64,512]{2,1,0:T(8,128)(2,1)}, u32[]{:S(2)}) copy-start(bf16[16,64,512]{2,1,0:T(8,128)(2,1)} %param.19) | copy-start | bytes 3145732
  6.5 115.1 %all-gather.4.cloned.1.call-start = ((), (), s32[]{:S(2)}) async-start(), calls=%async_computation.2 | async-start | bytes 1671168 | tf_op jit(solution)/shard_map/all_gather | solution.py:15
  6.5 17.2 %collective-permute-start = (bf16[1,1536]{1,0:T(2,128)(2,1)}, bf16[1,1536]{1,0:T(2,128)(2,1)S(1)}, u32[]{:S(2)}, u32[]{:S(2)}) collective-permute-start(bf16[1,1536]{1,0:T(2,128)(2,1)} %param.17), channel_id=1, source_target_pairs={{0,1},{1,2},{2,3},{3,4},{4,5},{5,6},{6,7},{7,8},{8,9},{9,10},{10,1... | collective-permute-start | bytes 9224 | tf_op jit(solution)/shard_map/ppermute | solution.py:75
  8.3 19.5 %collective-permute-start.1 = (bf16[1,1536]{1,0:T(2,128)(2,1)}, bf16[1,1536]{1,0:T(2,128)(2,1)S(1)}, u32[]{:S(2)}, u32[]{:S(2)}) collective-permute-start(bf16[1,1536]{1,0:T(2,128)(2,1)} %param.17), channel_id=1, source_target_pairs={{0,15},{1,0},{2,1},{3,2},{4,3},{5,4},{6,5},{7,6},{8,7},{9,8},{10,9... | collective-permute-start | bytes 9224 | tf_op jit(solution)/shard_map/ppermute | solution.py:80
  23.8 4.1 collective-permute-start.2
  27.8 4.0 collective-permute-start.3
  27.9 3.9 collective-permute-start.4
  31.8 4.0 collective-permute-start.5
  31.8 4.0 collective-permute-start.6
  35.8 4.0 collective-permute-start.7
  35.8 4.0 collective-permute-start.8
  39.7 4.0 collective-permute-start.9
  39.7 4.0 collective-permute-start.10
  43.7 4.0 collective-permute-start.11
  43.7 4.0 collective-permute-start.12
  47.6 10.2 %collective-permute-start.13 = (bf16[1,1536]{1,0:T(2,128)(2,1)S(1)}, bf16[1,1536]{1,0:T(2,128)(2,1)S(1)}, u32[]{:S(2)}, u32[]{:S(2)}) collective-permute-start(bf16[1,1536]{1,0:T(2,128)(2,1)S(1)} %collective-permute-done.11), channel_id=1, source_target_pairs={{0,15},{1,0},{2,1},{3,2},{4,3},{5,4},{6,5},{7,6},{8,7},{9,8},{10,9... | collective-permute-start | bytes 9224 | tf_op jit(solution)/shard_map/ppermute | solution.py:80
  47.6 10.3 %collective-permute-start.14 = (bf16[1,1536]{1,0:T(2,128)(2,1)S(1)}, bf16[1,1536]{1,0:T(2,128)(2,1)S(1)}, u32[]{:S(2)}, u32[]{:S(2)}) collective-permute-start(bf16[1,1536]{1,0:T(2,128)(2,1)S(1)} %collective-permute-done.12), channel_id=1, source_target_pairs={{0,1},{1,2},{2,3},{3,4},{4,5},{5,6},{6,7},{7,8},{8,9},{9,10},{10,1... | collective-permute-start | bytes 9224 | tf_op jit(solution)/shard_map/ppermute | solution.py:75
  50.3 6.0 %copy-start.6 = (bf16[1,1536]{1,0:T(2,128)(2,1)S(1)}, bf16[1,1536]{1,0:T(2,128)(2,1)}, u32[]{:S(2)}) copy-start(bf16[1,1536]{1,0:T(2,128)(2,1)} %param.17) | copy-start | bytes 9220
  58.8 6.7 %copy-start.5 = (s32[128,8]{0,1:T(8,128)S(1)}, s32[128,8]{0,1:T(8,128)}, u32[]{:S(2)}) copy-start(s32[128,8]{0,1:T(8,128)} %param.30) | copy-start | bytes 12292
  61.7 13.7 %copy-start.2 = (bf16[127,1536]{1,0:T(8,128)(2,1)S(1)}, bf16[127,1536]{1,0:T(8,128)(2,1)}, u32[]{:S(2)}) copy-start(bf16[127,1536]{1,0:T(8,128)(2,1)} %param.25) | copy-start | bytes 1170436
  61.7 13.9 %copy-start.4 = (f32[1536]{0:T(1024)S(1)}, f32[1536]{0:T(1024)}, u32[]{:S(2)}) copy-start(f32[1536]{0:T(1024)} %param.26) | copy-start | bytes 18436
  122.6 21.4 %copy-start.9 = (f32[24]{0:T(128)S(1)}, f32[24]{0:T(128)}, u32[]{:S(2)}) copy-start(f32[24]{0:T(128)} %param.22) | copy-start | bytes 292
  122.6 21.6 %copy-start.7 = (bf16[1,1536]{1,0:T(2,128)(2,1)S(1)}, bf16[1,1536]{1,0:T(2,128)(2,1)}, u32[]{:S(2)}) copy-start(bf16[1,1536]{1,0:T(2,128)(2,1)} %param.24) | copy-start | bytes 9220
  154.9 112.8 %copy-start.10 = (bf16[1,1536,512]{2,1,0:T(8,128)(2,1)S(1)}, bf16[1,1536,512]{2,1,0:T(8,128)(2,1)}, u32[]{:S(2)}) copy-start(bf16[1,1536,512]{2,1,0:T(8,128)(2,1)} %param.28) | copy-start | bytes 4718596
  265.5 2.2 copy-start.1
  281.5 5.2 %copy-start.8 = (f32[128,8]{0,1:T(8,128)S(1)}, f32[128,8]{0,1:T(8,128)}, u32[]{:S(2)}) copy-start(f32[128,8]{0,1:T(8,128)} %param.31) | copy-start | bytes 12292
  281.5 108.9 %all-to-all-start.1 = ((bf16[16,96,1536]{2,1,0:T(8,128)(2,1)}), bf16[16,96,1536]{2,1,0:T(8,128)(2,1)}, u32[]{:S(2)}, u32[]{:S(2)}) async-start(bf16[16,96,1536]{2,1,0:T(8,128)(2,1)} %convolution_convert_fusion), calls=%async_computation.1 | async-start | bytes 9437184 | tf_op jit(solution)/shard_map/all_to_all | solution.py:198
Sparse Core Ops, SparseCore 0:
  65.6 50.4 all-gather.3
